TPU v7x, 32 devices: a whole 2x2x4 slice. The times are simulated.
32 devices in a mesh: ens: 2 (over y), gy: 4 (over z), gx: 4 (over x, core).
Axes of the slice: x: 2, y: 2, z: 4, core: 2. Of those that a mesh axis runs over, the one named last changes fastest.
Arguments:
- base_stream: float32 [4, 32, 512], P('ens', 'gy', 'gx'), parts along dimension 0, may hold values from -6 to 6
- tangent_vectors: float32 [64, 2, 32, 512], P('ens', None, 'gy', 'gx'), parts along dimension 0, may hold values from -40 to 40, as said below
Outputs:
- basis_vectors: float32 [64, 2, 32, 512], P('ens', None, 'gy', 'gx'), parts along dimension 0
- upper_factor: float32 [64, 32], P('ens'), parts along dimension 0
There are 2 independent parts, one for each index of `ens`. A program takes and returns all parts, laid end to end along the dimension named above; each array names one. Nothing has to cross between parts.
Inputs may be any that keep to these rules, and one draw needn't show every extreme that they name: `tangent_vectors`: Real-valued; the vectors are linearly independent.
All inputs are finite; a program needn't handle non-finite values.
Results may differ from a plain program's by a relative error of at most 0.0003.
Values sent between devices are 32-bit elements; how exact they have to be, the bound alone decides.
A program may use at most 64 MiB of HBM per device.

v0:
```python
import jax
import jax.numpy as jnp
from jax import lax
from jax.sharding import PartitionSpec as P

coupling_top = 0.6
coupling_bottom = 0.3
time_step = 0.05
hyper_visc = 0.1


def padded(cells, sides, width):
    for axis, dim in sides:
        count = lax.axis_size(axis)
        head = lax.slice_in_dim(cells, 0, width, axis=dim)
        tail = lax.slice_in_dim(cells, cells.shape[dim] - width, cells.shape[dim], axis=dim)
        cells = jnp.concatenate(
            [
                lax.ppermute(tail, axis, [(i, (i + 1) % count) for i in range(count)]),
                cells,
                lax.ppermute(head, axis, [((i + 1) % count, i) for i in range(count)]),
            ],
            axis=dim,
        )
    return cells


def combined_all(value, axis, join):
    pieces = lax.all_gather(value, axis)
    head = pieces[0]
    tail = pieces[1:]
    running, _ = lax.scan(lambda running, slab: (join(running, slab), None), head, tail)
    return running


def inner_part(values):
    return values[..., 1:-1, 1:-1]


def padded_neighbours(values):
    return (
        values[..., 1:-1, :-2]
        + values[..., 1:-1, 2:]
        + values[..., :-2, 1:-1]
        + values[..., 2:, 1:-1]
    )


def padded_laplacian(values):
    return padded_neighbours(values) - 4.0 * inner_part(values)


def padded_cols(values):
    return values[..., 1:-1, 2:] - values[..., 1:-1, :-2]


def padded_rows(values):
    return values[..., 2:, 1:-1] - values[..., :-2, 1:-1]


def padded_jacobian(first, second):
    return (
        padded_cols(first) * padded_rows(second) - padded_rows(first) * padded_cols(second)
    ) * 0.25


def coupling_array():
    return jnp.array([coupling_top, coupling_bottom], jnp.float32).reshape(2, 1, 1)


def padded_relax(stream_ext, potential):
    coupling = coupling_array()
    return (
        padded_neighbours(stream_ext) + coupling * jnp.flip(inner_part(stream_ext), -3) - potential
    ) / (4.0 + coupling)


def pv_halo(potential):
    return padded(potential, (("gy", 2), ("gx", 3)), 2)


def combine_factors(left_factor, right_factor):
    summed = jnp.dot(
        left_factor.T,
        left_factor,
        precision=lax.Precision.HIGHEST,
        preferred_element_type=jnp.float32,
    )
    summed = summed + jnp.dot(
        right_factor.T,
        right_factor,
        precision=lax.Precision.HIGHEST,
        preferred_element_type=jnp.float32,
    )
    return jnp.linalg.cholesky(summed).T


def base_fields(base_ext):
    coupling = coupling_array()
    base_cycle = inner_part(base_ext)
    base_pv = padded_laplacian(base_ext) - coupling * (base_cycle - jnp.flip(base_cycle, -3))
    return (base_cycle, base_pv)


def tendency_of(pv_wide, stream_cycle, base_cycle, base_pv):
    pv_cycle = inner_part(pv_wide)
    return (
        -padded_jacobian(base_cycle, pv_cycle)
        - padded_jacobian(stream_cycle, base_pv)
        - hyper_visc * padded_laplacian(padded_laplacian(pv_wide))
    )


def local(base_stream, tangent_vectors):
    coupling = coupling_array()
    base_ext = padded(base_stream, (("gy", 1), ("gx", 2)), 2)
    base_cycle, base_pv = base_fields(base_ext)
    potential = tangent_vectors
    pv_wide = pv_halo(potential)
    stream_wide = -pv_wide / (4.0 + coupling)
    stream_cycle = padded_relax(stream_wide, inner_part(pv_wide))
    potential = potential + time_step * tendency_of(pv_wide, stream_cycle, base_cycle, base_pv)
    cells = potential.shape[1] * potential.shape[2] * potential.shape[3]
    total = 1.0 * cells * lax.axis_size("gy") * lax.axis_size("gx")
    columns = potential.reshape(potential.shape[0], cells)
    local_gram = (
        jnp.dot(
            columns, columns.T, precision=lax.Precision.HIGHEST, preferred_element_type=jnp.float32
        )
        / total
    )
    local_upper = jnp.linalg.cholesky(local_gram).T
    upper = combined_all(local_upper, ("gy", "gx"), combine_factors)
    lower = upper.T
    basis = lax.linalg.triangular_solve(lower, columns, left_side=True, lower=True)
    return (basis.reshape(potential.shape), upper)


def solution(mesh):
    return jax.shard_map(
        local,
        mesh=mesh,
        in_specs=(P("ens", "gy", "gx"), P("ens", None, "gy", "gx")),
        out_specs=(P("ens", None, "gy", "gx"), P("ens", None)),
        check_vma=False,
    )
```

profile of v0, /device:TPU:0, one launch (start us, length us, event | category | flops | bytes accessed | tf_op | source)
XLA Modules:
  0.0 134.5 jit_solution(5237825671170848654)
XLA Ops:
  0.6 0.8 fusion.40
  1.4 3.0 %collective-permute-start = (f32[2,2,128]{2,1,0:T(2,128)S(1)}, f32[2,2,128]{2,1,0:T(2,128)S(1)}, u32[]{:S(2)}, u32[]{:S(2)}) collective-permute-start(f32[2,2,128]{2,1,0:T(2,128)S(1)} %get-tuple-element.56), channel_id=1, source_target_pairs={{0,4},{4,8},{8,12},{12,0},{1,5},{5,9},{9,13},{13,1},{2,6},{6,10},{... | collective-permute-start | bytes 6152 | tf_op jit(solution)/shard_map/ppermute | solution.py:19
  4.4 2.0 %collective-permute-start.1 = (f32[2,2,128]{2,1,0:T(2,128)S(1)}, f32[2,2,128]{2,1,0:T(2,128)S(1)}, u32[]{:S(2)}, u32[]{:S(2)}) collective-permute-start(f32[2,2,128]{2,1,0:T(2,128)S(1)} %get-tuple-element.57), channel_id=1, source_target_pairs={{4,0},{8,4},{12,8},{0,12},{5,1},{9,5},{13,9},{1,13},{6,2},{10,6},{... | collective-permute-start | bytes 6152 | tf_op jit(solution)/shard_map/ppermute | solution.py:21
  6.5 1.1 fusion.38
  7.6 2.1 %collective-permute-start.4 = (f32[32,2,2,128]{3,2,1,0:T(2,128)S(1)}, f32[32,2,2,128]{3,2,1,0:T(2,128)S(1)}, u32[]{:S(2)}, u32[]{:S(2)}) collective-permute-start(f32[32,2,2,128]{3,2,1,0:T(2,128)S(1)} %get-tuple-element.49), channel_id=1, source_target_pairs={{4,0},{8,4},{12,8},{0,12},{5,1},{9,5},{13,9},{1,13},{6,2},{10,6},{... | collective-permute-start | bytes 196616 | tf_op jit(solution)/shard_map/ppermute | solution.py:21
  10.3 1.0 collective-permute-done.2
  11.3 1.7 %collective-permute-done.3 = f32[2,12,2]{2,1,0:T(8,128)S(1)} collective-permute-done((f32[2,12,2]{2,1,0:T(8,128)S(1)}, f32[2,12,2]{2,1,0:T(8,128)S(1)}, u32[]{:S(2)}, u32[]{:S(2)}) %collective-permute-start.3) | collective-permute-done | bytes 224 | tf_op jit(solution)/shard_map/ppermute | solution.py:19
  13.3 2.4 %collective-permute-done.5 = f32[32,2,2,128]{3,2,1,0:T(2,128)S(1)} collective-permute-done((f32[32,2,2,128]{3,2,1,0:T(2,128)S(1)}, f32[32,2,2,128]{3,2,1,0:T(2,128)S(1)}, u32[]{:S(2)}, u32[]{:S(2)}) %collective-permute-start.5) | collective-permute-done | bytes 65568 | tf_op jit(solution)/shard_map/ppermute | solution.py:19
  16.7 10.7 %collective-permute-done.6 = f32[32,2,12,2]{3,2,1,0:T(8,128)S(1)} collective-permute-done((f32[32,2,12,2]{3,2,1,0:T(8,128)S(1)}, f32[32,2,12,2]{3,2,1,0:T(8,128)S(1)}, u32[]{:S(2)}, u32[]{:S(2)}) %collective-permute-start.6) | collective-permute-done | bytes 6176 | tf_op jit(solution)/shard_map/ppermute | solution.py:21
  27.4 2.9 %collective-permute-done.7 = f32[32,2,12,2]{3,2,1,0:T(8,128)S(1)} collective-permute-done((f32[32,2,12,2]{3,2,1,0:T(8,128)S(1)}, f32[32,2,12,2]{3,2,1,0:T(8,128)S(1)}, u32[]{:S(2)}, u32[]{:S(2)}) %collective-permute-start.7) | collective-permute-done | bytes 6176 | tf_op jit(solution)/shard_map/ppermute | solution.py:19
  30.4 0.8 negate_multiply_fusion
  31.5 2.3 %fusion.9 = (f32[32,2,10,130]{3,2,1,0:T(8,128)S(1)}, f32[32,2,10,130]{3,2,1,0:T(8,128)S(1)}) fusion(f32[32,2,12,132]{3,2,1,0:T(8,128)S(1)} %get-tuple-element.42, f32[32,2,10,130]{3,2,1,0:T(8,128)S(1)} %slice.229, f32[32,2,12,132]{3,2,1,0:T(8,128)S(1)} %get-tuple-element.43, f32[2]{0:T(128)S(1)} %copy-done.3, f32[2]{0:T(128)S(1)} %copy-done.2, ...), kind=kLoop, calls=%fused_computation.26 | loop fusion | flops 1497600 | bytes 3733520 | tf_op jit(solution)/shard_map/div | solution.py:73
  33.8 1.0 fusion.14
  35.3 2.9 %cholesky.55 = f32[32,32]{1,0:T(8,128)S(1)} custom-call(f32[32,32]{1,0:T(8,128)S(1)} %fusion.35), custom_call_target="Cholesky" | custom-call | tf_op jit(solution)/shard_map/jit(cholesky)/cholesky | solution.py:132
  38.2 0.6 compare_reduce_fusion.1
  38.8 0.6 select_bitcast_fusion.1
  39.6 19.4 %all-gather = f32[512,32]{1,0:T(8,128)S(1)} all-gather(f32[32,32]{1,0:T(8,128)S(1)} %copy.37), channel_id=2, replica_groups=mesh['ens'=2,'gy'=4,'gx'=4] {'gy','gx'}, dimensions={0}, use_global_device_ids=true | all-gather | bytes 69632 | tf_op jit(solution)/shard_map/all_gather | solution.py:29
  59.1 70.9 %while.10 = (s32[]{:T(128)}, f32[32,32]{0,1:T(8,128)S(1)}, f32[15,32,32]{2,1,0:T(8,128)S(1)}, s32[]{:T(128)}) while((s32[]{:T(128)}, f32[32,32]{0,1:T(8,128)S(1)}, f32[15,32,32]{2,1,0:T(8,128)S(1)}, s32[]{:T(128)}) %tuple.42), condition=%wide.region_3.5_spmd, body=%wide.region_2.4_spmd.sunk | while | flops 795681 | bytes 78139 | solution.py:32
  59.5 2.9 %cholesky.118 = f32[32,32]{1,0:T(8,128)S(1)} custom-call(f32[32,32]{1,0:T(8,128)S(1)} %fusion.53), custom_call_target="Cholesky" | custom-call | tf_op jit(solution)/shard_map/while/body/eval_jaxpr/jit(cholesky)/cholesky | solution.py:95
  62.5 0.6 compare_reduce_fusion.3
  63.1 0.6 select_bitcast_fusion.3
  64.2 2.9 %cholesky.118 = f32[32,32]{1,0:T(8,128)S(1)} custom-call(f32[32,32]{1,0:T(8,128)S(1)} %fusion.53), custom_call_target="Cholesky" | custom-call | tf_op jit(solution)/shard_map/while/body/eval_jaxpr/jit(cholesky)/cholesky | solution.py:95
  67.2 0.6 compare_reduce_fusion.3
  67.8 0.6 select_bitcast_fusion.3
  69.0 2.9 %cholesky.118 = f32[32,32]{1,0:T(8,128)S(1)} custom-call(f32[32,32]{1,0:T(8,128)S(1)} %fusion.53), custom_call_target="Cholesky" | custom-call | tf_op jit(solution)/shard_map/while/body/eval_jaxpr/jit(cholesky)/cholesky | solution.py:95
  71.9 0.6 compare_reduce_fusion.3
  72.6 0.6 select_bitcast_fusion.3
  73.7 2.9 %cholesky.118 = f32[32,32]{1,0:T(8,128)S(1)} custom-call(f32[32,32]{1,0:T(8,128)S(1)} %fusion.53), custom_call_target="Cholesky" | custom-call | tf_op jit(solution)/shard_map/while/body/eval_jaxpr/jit(cholesky)/cholesky | solution.py:95
  76.7 0.6 compare_reduce_fusion.3
  77.3 0.6 select_bitcast_fusion.3
  78.4 2.9 %cholesky.118 = f32[32,32]{1,0:T(8,128)S(1)} custom-call(f32[32,32]{1,0:T(8,128)S(1)} %fusion.53), custom_call_target="Cholesky" | custom-call | tf_op jit(solution)/shard_map/while/body/eval_jaxpr/jit(cholesky)/cholesky | solution.py:95
  81.4 0.6 compare_reduce_fusion.3
  82.0 0.6 select_bitcast_fusion.3
  83.2 2.9 %cholesky.118 = f32[32,32]{1,0:T(8,128)S(1)} custom-call(f32[32,32]{1,0:T(8,128)S(1)} %fusion.53), custom_call_target="Cholesky" | custom-call | tf_op jit(solution)/shard_map/while/body/eval_jaxpr/jit(cholesky)/cholesky | solution.py:95
  86.1 0.6 compare_reduce_fusion.3
  86.7 0.6 select_bitcast_fusion.3
  87.9 2.9 %cholesky.118 = f32[32,32]{1,0:T(8,128)S(1)} custom-call(f32[32,32]{1,0:T(8,128)S(1)} %fusion.53), custom_call_target="Cholesky" | custom-call | tf_op jit(solution)/shard_map/while/body/eval_jaxpr/jit(cholesky)/cholesky | solution.py:95
  90.8 0.6 compare_reduce_fusion.3
  91.5 0.6 select_bitcast_fusion.3
  92.6 2.9 %cholesky.118 = f32[32,32]{1,0:T(8,128)S(1)} custom-call(f32[32,32]{1,0:T(8,128)S(1)} %fusion.53), custom_call_target="Cholesky" | custom-call | tf_op jit(solution)/shard_map/while/body/eval_jaxpr/jit(cholesky)/cholesky | solution.py:95
  95.6 0.6 compare_reduce_fusion.3
  96.2 0.6 select_bitcast_fusion.3
  97.3 2.9 %cholesky.118 = f32[32,32]{1,0:T(8,128)S(1)} custom-call(f32[32,32]{1,0:T(8,128)S(1)} %fusion.53), custom_call_target="Cholesky" | custom-call | tf_op jit(solution)/shard_map/while/body/eval_jaxpr/jit(cholesky)/cholesky | solution.py:95
  100.3 0.6 compare_reduce_fusion.3
  100.9 0.6 select_bitcast_fusion.3
  102.1 2.9 %cholesky.118 = f32[32,32]{1,0:T(8,128)S(1)} custom-call(f32[32,32]{1,0:T(8,128)S(1)} %fusion.53), custom_call_target="Cholesky" | custom-call | tf_op jit(solution)/shard_map/while/body/eval_jaxpr/jit(cholesky)/cholesky | solution.py:95
  105.0 0.6 compare_reduce_fusion.3
  105.6 0.6 select_bitcast_fusion.3
  106.8 2.9 %cholesky.118 = f32[32,32]{1,0:T(8,128)S(1)} custom-call(f32[32,32]{1,0:T(8,128)S(1)} %fusion.53), custom_call_target="Cholesky" | custom-call | tf_op jit(solution)/shard_map/while/body/eval_jaxpr/jit(cholesky)/cholesky | solution.py:95
  109.7 0.6 compare_reduce_fusion.3
  110.4 0.6 select_bitcast_fusion.3
  111.5 2.9 %cholesky.118 = f32[32,32]{1,0:T(8,128)S(1)} custom-call(f32[32,32]{1,0:T(8,128)S(1)} %fusion.53), custom_call_target="Cholesky" | custom-call | tf_op jit(solution)/shard_map/while/body/eval_jaxpr/jit(cholesky)/cholesky | solution.py:95
  114.5 0.6 compare_reduce_fusion.3
  115.1 0.6 select_bitcast_fusion.3
  116.2 2.9 %cholesky.118 = f32[32,32]{1,0:T(8,128)S(1)} custom-call(f32[32,32]{1,0:T(8,128)S(1)} %fusion.53), custom_call_target="Cholesky" | custom-call | tf_op jit(solution)/shard_map/while/body/eval_jaxpr/jit(cholesky)/cholesky | solution.py:95
  119.2 0.6 compare_reduce_fusion.3
  119.8 0.6 select_bitcast_fusion.3
  121.0 2.9 %cholesky.118 = f32[32,32]{1,0:T(8,128)S(1)} custom-call(f32[32,32]{1,0:T(8,128)S(1)} %fusion.53), custom_call_target="Cholesky" | custom-call | tf_op jit(solution)/shard_map/while/body/eval_jaxpr/jit(cholesky)/cholesky | solution.py:95
  124.5 0.6 select_bitcast_fusion.3
  125.7 2.9 %cholesky.118 = f32[32,32]{1,0:T(8,128)S(1)} custom-call(f32[32,32]{1,0:T(8,128)S(1)} %fusion.53), custom_call_target="Cholesky" | custom-call | tf_op jit(solution)/shard_map/while/body/eval_jaxpr/jit(cholesky)/cholesky | solution.py:95
  129.3 0.6 select_bitcast_fusion.3
  130.0 0.7 copy.44
  130.6 2.4 %custom-call.5 = f32[1,32,32]{1,2,0:T(8,128)S(1)} custom-call(f32[1,32,32]{2,1,0:T(8,128)S(1)} %fusion.34), custom_call_target="InvertDiagBlocksLowerTriangular" | custom-call | tf_op jit(solution)/shard_map/triangular_solve | solution.py:135
  133.7 0.9 copy.43
  (114 shorter events, 11.8 us)
Async XLA Ops:
  1.4 8.3 %collective-permute-start = (f32[2,2,128]{2,1,0:T(2,128)S(1)}, f32[2,2,128]{2,1,0:T(2,128)S(1)}, u32[]{:S(2)}, u32[]{:S(2)}) collective-permute-start(f32[2,2,128]{2,1,0:T(2,128)S(1)} %get-tuple-element.56), channel_id=1, source_target_pairs={{0,4},{4,8},{8,12},{12,0},{1,5},{5,9},{9,13},{13,1},{2,6},{6,10},{... | collective-permute-start | bytes 6152 | tf_op jit(solution)/shard_map/ppermute | solution.py:19
  4.4 5.2 %collective-permute-start.1 = (f32[2,2,128]{2,1,0:T(2,128)S(1)}, f32[2,2,128]{2,1,0:T(2,128)S(1)}, u32[]{:S(2)}, u32[]{:S(2)}) collective-permute-start(f32[2,2,128]{2,1,0:T(2,128)S(1)} %get-tuple-element.57), channel_id=1, source_target_pairs={{4,0},{8,4},{12,8},{0,12},{5,1},{9,5},{13,9},{1,13},{6,2},{10,6},{... | collective-permute-start | bytes 6152 | tf_op jit(solution)/shard_map/ppermute | solution.py:21
  6.5 3.2 %copy-start.1 = (f32[2,8,128]{2,1,0:T(8,128)S(1)}, f32[2,8,128]{2,1,0:T(8,128)}, u32[]{:S(2)}) copy-start(f32[2,8,128]{2,1,0:T(8,128)} %param.8) | copy-start | bytes 24580
  6.5 6.7 %copy-start.2 = (f32[2]{0:T(128)S(1)}, f32[2]{0:T(128)}, u32[]{:S(2)}) copy-start(f32[2]{0:T(128)} %constant.56.clone) | copy-start | bytes 28
  7.6 8.2 %copy-start = (f32[32,2,8,128]{3,2,1,0:T(8,128)S(1)}, f32[32,2,8,128]{3,2,1,0:T(8,128)}, u32[]{:S(2)}) copy-start(f32[32,2,8,128]{3,2,1,0:T(8,128)} %param.9) | copy-start | bytes 786436
  7.6 5.8 %collective-permute-start.4 = (f32[32,2,2,128]{3,2,1,0:T(2,128)S(1)}, f32[32,2,2,128]{3,2,1,0:T(2,128)S(1)}, u32[]{:S(2)}, u32[]{:S(2)}) collective-permute-start(f32[32,2,2,128]{3,2,1,0:T(2,128)S(1)} %get-tuple-element.49), channel_id=1, source_target_pairs={{4,0},{8,4},{12,8},{0,12},{5,1},{9,5},{13,9},{1,13},{6,2},{10,6},{... | collective-permute-start | bytes 196616 | tf_op jit(solution)/shard_map/ppermute | solution.py:21
  9.7 6.1 %collective-permute-start.5 = (f32[32,2,2,128]{3,2,1,0:T(2,128)S(1)}, f32[32,2,2,128]{3,2,1,0:T(2,128)S(1)}, u32[]{:S(2)}, u32[]{:S(2)}) collective-permute-start(f32[32,2,2,128]{3,2,1,0:T(2,128)S(1)} %get-tuple-element.48), channel_id=1, source_target_pairs={{0,4},{4,8},{8,12},{12,0},{1,5},{5,9},{9,13},{13,1},{2,6},{6,10},{... | collective-permute-start | bytes 196616 | tf_op jit(solution)/shard_map/ppermute | solution.py:19
  9.8 1.5 %collective-permute-start.2 = (f32[2,12,2]{2,1,0:T(8,128)S(1)}, f32[2,12,2]{2,1,0:T(8,128)S(1)}, u32[]{:S(2)}, u32[]{:S(2)}) collective-permute-start(f32[2,12,2]{2,1,0:T(8,128)S(1)} %get-tuple-element.53), channel_id=1, source_target_pairs={{1,0},{2,1},{3,2},{0,3},{5,4},{6,5},{7,6},{4,7},{9,8},{10,9},{11,1... | collective-permute-start | bytes 584 | tf_op jit(solution)/shard_map/ppermute | solution.py:21
  9.9 3.2 %collective-permute-start.3 = (f32[2,12,2]{2,1,0:T(8,128)S(1)}, f32[2,12,2]{2,1,0:T(8,128)S(1)}, u32[]{:S(2)}, u32[]{:S(2)}) collective-permute-start(f32[2,12,2]{2,1,0:T(8,128)S(1)} %get-tuple-element.52), channel_id=1, source_target_pairs={{0,1},{1,2},{2,3},{3,0},{4,5},{5,6},{6,7},{7,4},{8,9},{9,10},{10,1... | collective-permute-start | bytes 584 | tf_op jit(solution)/shard_map/ppermute | solution.py:19
  16.0 11.4 %collective-permute-start.6 = (f32[32,2,12,2]{3,2,1,0:T(8,128)S(1)}, f32[32,2,12,2]{3,2,1,0:T(8,128)S(1)}, u32[]{:S(2)}, u32[]{:S(2)}) collective-permute-start(f32[32,2,12,2]{3,2,1,0:T(8,128)S(1)} %get-tuple-element.47), channel_id=1, source_target_pairs={{1,0},{2,1},{3,2},{0,3},{5,4},{6,5},{7,6},{4,7},{9,8},{10,9},{11,1... | collective-permute-start | bytes 18440 | tf_op jit(solution)/shard_map/ppermute | solution.py:21
  16.1 14.3 %copy-start.3 = (f32[2]{0:T(128)S(1)}, f32[2]{0:T(128)}, u32[]{:S(2)}) copy-start(f32[2]{0:T(128)} %constant.58) | copy-start | bytes 28
  16.1 14.2 %collective-permute-start.7 = (f32[32,2,12,2]{3,2,1,0:T(8,128)S(1)}, f32[32,2,12,2]{3,2,1,0:T(8,128)S(1)}, u32[]{:S(2)}, u32[]{:S(2)}) collective-permute-start(f32[32,2,12,2]{3,2,1,0:T(8,128)S(1)} %get-tuple-element.46), channel_id=1, source_target_pairs={{0,1},{1,2},{2,3},{3,0},{4,5},{5,6},{6,7},{7,4},{8,9},{9,10},{10,1... | collective-permute-start | bytes 18440 | tf_op jit(solution)/shard_map/ppermute | solution.py:19
where the time goes:
time: 135 us
  other arithmetic  74.9 us (55%)
  blocking collectives  19.4 us (14%)
  waiting for transfers between devices  18.8 us (14%)
  starting transfers between devices  8.18 us (6%)
  matrix products  6.21 us (5%)
  local copies, waits for them, and re-layouts  5.6 us (4%)
    another operation x45, other arithmetic, combine_factors(): return jnp.linalg.cholesky(summed).T  53.9 us
    all_gather x1, blocking collectives, combined_all(): pieces = lax.all_gather(value, axis)  19.4 us
    ppermute x4, waiting for transfers between devices, padded(): lax.ppermute(head, axis, [((i + 1) % count, i) for i in range(count)])  11.8 us
    transpose x15, other arithmetic, combine_factors(): return jnp.linalg.cholesky(summed).T  9.74 us
    ppermute x4, waiting for transfers between devices, padded(): lax.ppermute(tail, axis, [(i, (i + 1) % count) for i in range(count)])  7.05 us
    ppermute x4, starting transfers between devices, padded(): lax.ppermute(head, axis, [((i + 1) % count, i) for i in range(count)])  4.25 us
    ppermute x4, starting transfers between devices, padded(): lax.ppermute(tail, axis, [(i, (i + 1) % count) for i in range(count)])  3.93 us
    another operation x3, other arithmetic, local(): local_upper = jnp.linalg.cholesky(local_gram).T  3.6 us
  transfers between devices with their start and end apart: 8, of which 5 were waited for; matrix products, arithmetic and copies ran while one was open for 1% of the time, Pallas kernels for 0%

commit v1 on v0

v1 whole, which is shorter than its diff:
```python
import functools

import jax
import jax.numpy as jnp
from jax import lax
from jax.experimental import pallas as pl
from jax.experimental.pallas import tpu as pltpu
from jax.sharding import PartitionSpec as P

coupling = (0.6, 0.3)
time_step = 0.05
hyper_visc = 0.1
halo = 2
MESH = pl.DeviceIdType.MESH
SUB = 8


def lanes_of(shape):
    return lax.broadcasted_iota(jnp.int32, shape, 1)


def rows_of(shape):
    return lax.broadcasted_iota(jnp.int32, shape, 0)


def turn(values, shift, axis=1):
    size = values.shape[axis]
    shift = shift % size
    return values if shift == 0 else pltpu.roll(values, shift, axis)


def base_coefficients(base, coef_ref):
    rows, cols = base[1][1][0].shape
    tall = [[jnp.concatenate([base[y][x][l] for y in range(3)], 0) for l in range(2)] for x in range(3)]
    lane = lanes_of((3 * rows, cols))
    here = tall[1]
    east = [turn(jnp.where(lane == 0, tall[2][l], here[l]), -1) for l in range(2)]
    east2 = [turn(jnp.where(lane < 2, tall[2][l], here[l]), -2) for l in range(2)]
    west = [turn(jnp.where(lane == cols - 1, tall[0][l], here[l]), 1) for l in range(2)]
    west2 = [turn(jnp.where(lane >= cols - 2, tall[0][l], here[l]), 2) for l in range(2)]

    def updown(v):
        return turn(v, 1, 0) + turn(v, -1, 0)

    def drow(v):
        return turn(v, -1, 0) - turn(v, 1, 0)

    for l in range(2):
        c, other = coupling[l], coupling[1 - l]
        alpha, beta = 1.0 / (4.0 + c), c / (4.0 + other)

        def pv(side, near):
            return near + updown(side[l]) - 4.0 * side[l] - c * (side[l] - side[1 - l])

        pv_here = pv(here, east[l] + west[l])
        pv_east = pv(east, east2[l] + here[l])
        pv_west = pv(west, west2[l] + here[l])
        quarter = time_step * 0.25
        a = quarter * (east[l] - west[l])
        b = quarter * drow(here[l])
        cc = quarter * (pv_east - pv_west)
        d = quarter * drow(pv_here)
        fields = (
            b + alpha * d,
            -a - alpha * cc,
            alpha * alpha * d,
            -alpha * alpha * cc,
            alpha * beta * d,
            -alpha * beta * cc,
        )
        for i, field in enumerate(fields):
            coef_ref[i, l] = field[rows : 2 * rows]


def evolve_kernel(
    gy, gx, base_ref, tangent_ref, evolved_ref, gram_ref,
    wide, coef, edge_out, edge_in, gram_out, gram_in,
    edge_send, edge_recv, row_send, row_recv, gram_send, gram_recv,
):
    layers, rows, cols = base_ref.shape
    vectors = tangent_ref.shape[0] // (layers * rows)
    my_y, my_x = lax.axis_index("gy"), lax.axis_index("gx")
    count = gy * gx
    me = my_y * gx + my_x

    def partner(step):
        at = lax.rem(me + step, count)
        return at, {"gy": at // gx, "gx": lax.rem(at, gx)}

    def each_partner(body):
        if count <= 32:
            for step in range(1, count):
                body(step)
        else:
            pl.loop(1, count)(body)

    barrier = pltpu.get_barrier_semaphore()
    each_partner(
        lambda step: pl.semaphore_signal(
            barrier, inc=1, device_id=partner(step)[1], device_id_type=MESH
        )
    )

    lane = lanes_of((vectors, cols))
    packed = jnp.zeros((vectors, cols), jnp.float32)
    for l in range(layers):
        for r in range(rows):
            slab = tangent_ref[pl.ds(l * rows + r, vectors, stride=layers * rows), :]
            wide[r + halo, l] = slab
            at = 2 * halo * (l * rows + r)
            packed = jnp.where((lane >= at) & (lane < at + 2 * halo), turn(slab, at + halo), packed)
    used = 2 * halo * layers * rows
    fold = cols // used
    groups = vectors // SUB
    tiles = groups // fold
    lane8 = lanes_of((SUB, cols))
    for t in range(tiles):
        tile = packed[t * fold * SUB : t * fold * SUB + SUB]
        for f in range(1, fold):
            g = t * fold + f
            tile = jnp.where(lane8 >= f * used, turn(packed[g * SUB : (g + 1) * SUB], f * used), tile)
        edge_out[t] = tile
    for l in range(layers):
        edge_out[tiles + l] = base_ref[l]

    pl.semaphore_wait(barrier, count - 1)

    def neighbour(dy, dx):
        return {"gy": lax.rem(my_y + dy + gy, gy), "gx": lax.rem(my_x + dx + gx, gx)}

    sides = [(0, -1), (0, 1), (-1, 0), (1, 0), (-1, -1), (-1, 1), (1, -1), (1, 1)]
    edges = []
    for dy, dx in sides:
        slot = (1 - dy) * 3 + 1 - dx
        copy = pltpu.make_async_remote_copy(
            src_ref=edge_out, dst_ref=edge_in.at[slot],
            send_sem=edge_send.at[slot], recv_sem=edge_recv.at[slot],
            device_id=neighbour(dy, dx), device_id_type=MESH,
        )
        copy.start()
        edges.append(copy)
    north = pltpu.make_async_remote_copy(
        src_ref=wide.at[pl.ds(halo, halo)], dst_ref=wide.at[pl.ds(rows + halo, halo)],
        send_sem=row_send.at[0], recv_sem=row_recv.at[0],
        device_id=neighbour(-1, 0), device_id_type=MESH,
    )
    south = pltpu.make_async_remote_copy(
        src_ref=wide.at[pl.ds(rows, halo)], dst_ref=wide.at[pl.ds(0, halo)],
        send_sem=row_send.at[1], recv_sem=row_recv.at[1],
        device_id=neighbour(1, 0), device_id_type=MESH,
    )
    north.start()
    south.start()
    for copy in edges:
        copy.wait_recv()

    base = [
        [
            [base_ref[l] if (y, x) == (1, 1) else edge_in[y * 3 + x, tiles + l] for l in range(layers)]
            for x in range(3)
        ]
        for y in range(3)
    ]
    base_coefficients(base, coef)

    from_east = lax.rem(lane, 2 * halo) >= halo
    spread = []
    for y in range(3):
        merged = []
        for t in range(tiles):
            tile = jnp.where(lax.rem(lane8, 2 * halo) >= halo, edge_in[y * 3 + 2, t], edge_in[y * 3, t])
            for f in range(fold):
                merged.append(turn(tile, -f * used))
        spread.append(jnp.concatenate(merged, 0))

    shifted = {}

    def shift(e, l):
        if (e, l) not in shifted:
            own = wide[e, l]
            r = e - halo
            y = 0 if r < 0 else (2 if r >= rows else 1)
            z = turn(spread[y], -(2 * halo * (l * rows + r % rows) + halo))
            near = (
                turn(jnp.where(lane == 0, z, own), -1),
                turn(jnp.where(lane == cols - 1, z, own), 1),
            )
            if y == 1:
                near = near + (
                    turn(jnp.where(lane < 2, z, own), -2),
                    turn(jnp.where(lane >= cols - 2, z, own), 2),
                )
            shifted[e, l] = near
        return shifted[e, l]

    sums = {}

    def near_sum(e, l):
        if (e, l) not in sums:
            side = shift(e, l)
            sums[e, l] = side[0] + side[1] + wide[e - 1, l] + wide[e + 1, l]
        return sums[e, l]

    def evolve_row(r):
        e = r + halo
        for l in range(layers):
            own = wide[e, l]
            east, west, east2, west2 = shift(e, l)
            up, down = shift(e - 1, l), shift(e + 1, l)
            sum_east = east2 + own + up[0] + down[0]
            sum_west = west2 + own + up[1] + down[1]
            sum_up, sum_down, here = near_sum(e - 1, l), near_sum(e + 1, l), near_sum(e, l)
            double = (sum_east + sum_west) + (sum_up + sum_down) - 8.0 * here + 16.0 * own
            other = shift(e, 1 - l)
            c = [coef[i, l, pl.ds(r, 1), :] for i in range(6)]
            result = own - (hyper_visc * time_step) * double
            result = result + c[0] * (east - west)
            result = result + c[1] * (wide[e + 1, l] - wide[e - 1, l])
            result = result + c[2] * (sum_east - sum_west)
            result = result + c[3] * (sum_down - sum_up)
            result = result + c[4] * (other[0] - other[1])
            result = result + c[5] * (wide[e + 1, 1 - l] - wide[e - 1, 1 - l])
            evolved_ref[r, l] = result

    middle = [r for r in range(halo, rows - halo)]
    for r in middle:
        evolve_row(r)
    north.wait_recv()
    south.wait_recv()
    for r in range(rows):
        if r not in middle:
            evolve_row(r)

    copies = cols // vectors
    gram = jnp.zeros((vectors, cols), jnp.float32)
    for r in range(rows):
        slab = jnp.concatenate([evolved_ref[r, l] for l in range(layers)], 1)
        gram = gram + lax.dot_general(
            slab, jnp.concatenate([slab] * copies, 0), (((1,), (1,)), ((), ())),
            precision=lax.Precision.HIGHEST, preferred_element_type=jnp.float32,
        )
    tile = gram[0:SUB]
    for g in range(1, groups):
        tile = jnp.where(lane8 >= g * vectors, gram[g * SUB : (g + 1) * SUB], tile)
    gram_out[...] = tile

    def gram_copy(step):
        at, device = partner(step)
        return pltpu.make_async_remote_copy(
            src_ref=gram_out, dst_ref=gram_in.at[me],
            send_sem=gram_send.at[at], recv_sem=gram_recv.at[me],
            device_id=device, device_id_type=MESH,
        )

    def gram_arrival(step):
        at, device = partner(step)
        return pltpu.make_async_remote_copy(
            src_ref=gram_out, dst_ref=gram_in.at[at],
            send_sem=gram_send.at[at], recv_sem=gram_recv.at[at],
            device_id=device, device_id_type=MESH,
        )

    each_partner(lambda step: gram_copy(step).start())
    gram_in[me] = tile
    for copy in edges:
        copy.wait_send()
    north.wait_send()
    south.wait_send()
    each_partner(lambda step: gram_arrival(step).wait_recv())
    total = gram_in[0]
    for i in range(1, count):
        total = total + gram_in[i]
    gram_ref[...] = total / (1.0 * layers * rows * cols * count)
    each_partner(lambda step: gram_copy(step).wait_send())


def basis_kernel(gram_ref, evolved_ref, basis_ref, upper_ref):
    rows, layers, vectors, cols = evolved_ref.shape
    groups = vectors // SUB
    tile = gram_ref[...]
    work = jnp.concatenate([turn(tile, -g * vectors) for g in range(groups)], 0)
    lane, row = lanes_of((vectors, cols)), rows_of((vectors, cols))
    work = jnp.where(lane < vectors, work, jnp.where(lane == row + vectors, 1.0, 0.0))
    for j in range(vectors):
        line = work[j : j + 1]
        scaled = line / work[j : j + 1, j : j + 1]
        work = work - jnp.where(row > j, work[:, j : j + 1], 0.0) * scaled
    diagonal = jnp.sum(jnp.where(lane == row, work, 0.0), axis=1, keepdims=True)
    work = work * lax.rsqrt(diagonal)
    upper_ref[...] = jnp.where(lane >= row, work, 0.0)[:, :vectors]
    inverse = turn(work, -vectors)[:, :vectors]
    for r in range(rows):
        slab = jnp.concatenate([evolved_ref[r, l] for l in range(layers)], 1)
        basis = lax.dot_general(
            inverse, slab, (((1,), (0,)), ((), ())),
            precision=lax.Precision.HIGHEST, preferred_element_type=jnp.float32,
        )
        for l in range(layers):
            basis_ref[pl.ds(l * rows + r, vectors, stride=layers * rows), :] = basis[
                :, l * cols : (l + 1) * cols
            ]


def solution(mesh):
    gy, gx = mesh.shape["gy"], mesh.shape["gx"]
    vmem = pl.BlockSpec(memory_space=pltpu.VMEM)

    def local(base_stream, tangent_vectors):
        vectors, layers, rows, cols = tangent_vectors.shape
        count = gy * gx
        f32 = jnp.float32
        tiles = vectors // SUB * 2 * halo * layers * rows // cols
        edge = (tiles + layers, SUB, cols)
        evolved, gram = pl.pallas_call(
            functools.partial(evolve_kernel, gy, gx),
            out_shape=(
                jax.ShapeDtypeStruct((rows, layers, vectors, cols), f32),
                jax.ShapeDtypeStruct((SUB, cols), f32),
            ),
            in_specs=[vmem, vmem],
            out_specs=(vmem, vmem),
            scratch_shapes=[
                pltpu.VMEM((rows + 2 * halo, layers, vectors, cols), f32),
                pltpu.VMEM((6, layers, rows, cols), f32),
                pltpu.VMEM(edge, f32),
                pltpu.VMEM((9,) + edge, f32),
                pltpu.VMEM((SUB, cols), f32),
                pltpu.VMEM((count, SUB, cols), f32),
                pltpu.SemaphoreType.DMA((9,)),
                pltpu.SemaphoreType.DMA((9,)),
                pltpu.SemaphoreType.DMA((2,)),
                pltpu.SemaphoreType.DMA((2,)),
                pltpu.SemaphoreType.DMA((count,)),
                pltpu.SemaphoreType.DMA((count,)),
            ],
            compiler_params=pltpu.CompilerParams(
                collective_id=0, has_side_effects=True, vmem_limit_bytes=32 * 1024 * 1024
            ),
            name="evolve",
        )(base_stream, tangent_vectors.reshape(vectors * layers * rows, cols))
        basis, upper = pl.pallas_call(
            basis_kernel,
            out_shape=(
                jax.ShapeDtypeStruct((vectors * layers * rows, cols), f32),
                jax.ShapeDtypeStruct((vectors, vectors), f32),
            ),
            in_specs=[vmem, vmem],
            out_specs=(vmem, vmem),
            compiler_params=pltpu.CompilerParams(vmem_limit_bytes=32 * 1024 * 1024),
            name="basis",
        )(gram, evolved)
        return basis.reshape(tangent_vectors.shape), upper

    return jax.shard_map(
        local,
        mesh=mesh,
        in_specs=(P("ens", "gy", "gx"), P("ens", None, "gy", "gx")),
        out_specs=(P("ens", None, "gy", "gx"), P("ens", None)),
        check_vma=False,
    )
```

time: 135 us -> 24.5 us (0.18)
  other arithmetic: 74.9 us -> 0 us
  Pallas kernels: 0 us -> 22 us
  blocking collectives: 19.4 us -> 0 us
  waiting for transfers between devices: 18.8 us -> 0 us
  starting transfers between devices: 8.18 us -> 0 us
  matrix products: 6.21 us -> 0 us
  local copies, waits for them, and re-layouts: 5.6 us -> 1.64 us
    another operation x50 -> x0, other arithmetic: 60 us -> none  [the longest x45 53.9 us: combine_factors(): return jnp.linalg.cholesky(summed).T]
    pallas_call x0 -> x2, Pallas kernels: none -> 22 us  [the longest x1 18.1 us: local(): pl.pallas_call(functools.partial(evolve_kernel, gy, gx), out_shape=(jax.S...]
    all_gather x1 -> x0, blocking collectives: 19.4 us -> none  [combined_all(): pieces = lax.all_gather(value, axis)]
    ppermute x8 -> x0, waiting for transfers between devices: 18.8 us -> none  [the longest x4 11.8 us: padded(): lax.ppermute(head, axis, [((i + 1) % count, i) for i in range(count)])]
    transpose x16 -> x0, other arithmetic: 10.4 us -> none  [the longest x15 9.74 us: combine_factors(): return jnp.linalg.cholesky(summed).T]
    ppermute x8 -> x0, starting transfers between devices: 8.18 us -> none  [the longest x4 4.25 us: padded(): lax.ppermute(head, axis, [((i + 1) % count, i) for i in range(count)])]
    dot_general x31 -> x0, matrix products: 5.8 us -> none  [the longest x15 3.24 us: combine_factors(): jnp.dot(right_factor.T, right_factor, precision=lax.Precision.HIGHEST, pr...]
    div x18 -> x0, other arithmetic: 3.19 us -> none  [the longest x1 2.3 us: padded_relax(): (padded_neighbours(stream_ext) + coupling * jnp.flip(inner_part(stream_ex...]
  transfers between devices with their start and end apart: 8 -> 0, of which waited for: 5 -> 0; matrix products, arithmetic and copies ran while one was open for 1% -> 0% of each run, Pallas kernels for 0% -> 0%
where the time goes in v1:
time: 24.5 us; the launch traced here: 24.3 us
  Pallas kernels  22 us (90%)
  local copies, waits for them, and re-layouts  1.64 us (7%)
  between operations  0.65 us (3%)
    pallas_call x1, Pallas kernels, local(): pl.pallas_call(functools.partial(evolve_kernel, gy, gx), out_shape=(jax.S...  18.1 us
    pallas_call x1, Pallas kernels, local(): pl.pallas_call(basis_kernel, out_shape=(jax.ShapeDtypeStruct((vectors * l...  3.83 us
    unnamed x4, local copies, waits for them, and re-layouts  1.64 us

profile of v1, /device:TPU:0, one launch (start us, length us, event | category | flops | bytes accessed | tf_op | source)
XLA Modules:
  0.0 24.3 jit_solution(7056597805675459520)
XLA Ops:
  0.6 0.0 copy-start
  0.6 0.9 %copy-done = f32[32,2,8,128]{3,2,1,0:T(8,128)S(1)} copy-done((f32[32,2,8,128]{3,2,1,0:T(8,128)S(1)}, f32[32,2,8,128]{3,2,1,0:T(8,128)}, u32[]{:S(2)}) %copy-start) | copy-done | bytes 262168
  1.6 0.0 copy-start.1
  1.6 0.7 %copy-done.1 = f32[2,8,128]{2,1,0:T(8,128)S(1)} copy-done((f32[2,8,128]{2,1,0:T(8,128)S(1)}, f32[2,8,128]{2,1,0:T(8,128)}, u32[]{:S(2)}) %copy-start.1) | copy-done | bytes 8216
  2.3 18.1 %evolve.1 = (f32[8,2,32,128]{3,2,1,0:T(8,128)S(1)}, f32[8,128]{1,0:T(8,128)S(1)}) custom-call(f32[2,8,128]{2,1,0:T(8,128)S(1)} %copy-done.1, f32[512,128]{1,0:T(8,128)S(1)} %bitcast.2), custom_call_target="tpu_custom_call" | custom-call | tf_op jit(solution)/shard_map/evolve/pallas_call | solution.py:314
  20.4 3.8 %basis.1 = (f32[512,128]{1,0:T(8,128)}, f32[32,32]{1,0:T(8,128)}) custom-call(f32[8,128]{1,0:T(8,128)S(1)} %get-tuple-element.6.gram_ref, f32[8,2,32,128]{3,2,1,0:T(8,128)S(1)} %get-tuple-element.7.evolved_ref), custom_call_target="tpu_custom_call" | custom-call | tf_op jit(solution)/shard_map/basis/pallas_call | solution.py:341
Async XLA Ops:
  0.6 1.0 %copy-start = (f32[32,2,8,128]{3,2,1,0:T(8,128)S(1)}, f32[32,2,8,128]{3,2,1,0:T(8,128)}, u32[]{:S(2)}) copy-start(f32[32,2,8,128]{3,2,1,0:T(8,128)} %param.3) | copy-start | bytes 786436
  1.6 0.7 %copy-start.1 = (f32[2,8,128]{2,1,0:T(8,128)S(1)}, f32[2,8,128]{2,1,0:T(8,128)}, u32[]{:S(2)}) copy-start(f32[2,8,128]{2,1,0:T(8,128)} %base_ref.1) | copy-start | bytes 24580

commit v2 on v1

--- a/solution.py
+++ b/solution.py
@@ -74,10 +74,11 @@
 
 def evolve_kernel(
     gy, gx, base_ref, tangent_ref, evolved_ref, gram_ref,
-    wide, coef, edge_out, edge_in, gram_out, gram_in,
-    edge_send, edge_recv, row_send, row_recv, gram_send, gram_recv,
+    tangent, wide, coef, edge_out, edge_in, corner_out, corner_in, base_in, gram_out, gram_in,
+    load_sem, edge_send, edge_recv, row_send, row_recv, gram_send, gram_recv,
 ):
     layers, rows, cols = base_ref.shape
+    tiles = edge_out.shape[0] - layers
     vectors = tangent_ref.shape[0] // (layers * rows)
     my_y, my_x = lax.axis_index("gy"), lax.axis_index("gx")
     count = gy * gx
@@ -101,18 +102,23 @@
         )
     )
 
+    fetch_vectors = pltpu.make_async_copy(tangent_ref, tangent, load_sem.at[0])
+    fetch_base = pltpu.make_async_copy(base_ref, edge_out.at[pl.ds(tiles, layers)], load_sem.at[1])
+    fetch_vectors.start()
+    fetch_base.start()
+    fetch_vectors.wait()
+
     lane = lanes_of((vectors, cols))
     packed = jnp.zeros((vectors, cols), jnp.float32)
     for l in range(layers):
         for r in range(rows):
-            slab = tangent_ref[pl.ds(l * rows + r, vectors, stride=layers * rows), :]
+            slab = tangent[pl.ds(l * rows + r, vectors, stride=layers * rows), :]
             wide[r + halo, l] = slab
             at = 2 * halo * (l * rows + r)
             packed = jnp.where((lane >= at) & (lane < at + 2 * halo), turn(slab, at + halo), packed)
     used = 2 * halo * layers * rows
     fold = cols // used
     groups = vectors // SUB
-    tiles = groups // fold
     lane8 = lanes_of((SUB, cols))
     for t in range(tiles):
         tile = packed[t * fold * SUB : t * fold * SUB + SUB]
@@ -120,25 +126,45 @@
             g = t * fold + f
             tile = jnp.where(lane8 >= f * used, turn(packed[g * SUB : (g + 1) * SUB], f * used), tile)
         edge_out[t] = tile
+    corner = jnp.zeros((SUB, cols), jnp.float32)
+    fetch_base.wait()
+
+    def corner_at(y, g, l):
+        return (((y // 2) * groups + g) * layers + l) * 2 * halo
+
+    def place(tile, at, values):
+        return jnp.where((lane8 >= at) & (lane8 < at + 2 * halo), turn(values, at + halo), tile)
+
+    base_at = 2 * groups * layers * 2 * halo
     for l in range(layers):
-        edge_out[tiles + l] = base_ref[l]
+        for y, r in ((2, 0), (0, rows - 1)):
+            for g in range(groups):
+                corner = place(corner, corner_at(y, g, l), wide[r + halo, l, pl.ds(g * SUB, SUB)])
+        corner = place(corner, base_at + l * 2 * halo, edge_out[tiles + l])
+    corner_out[...] = corner
 
     pl.semaphore_wait(barrier, count - 1)
 
     def neighbour(dy, dx):
         return {"gy": lax.rem(my_y + dy + gy, gy), "gx": lax.rem(my_x + dx + gx, gx)}
 
-    sides = [(0, -1), (0, 1), (-1, 0), (1, 0), (-1, -1), (-1, 1), (1, -1), (1, 1)]
+    def send(source, target, slot, dy, dx):
+        copy = pltpu.make_async_remote_copy(
+            src_ref=source, dst_ref=target, send_sem=edge_send.at[slot], recv_sem=edge_recv.at[slot],
+            device_id=neighbour(dy, dx), device_id_type=MESH,
+        )
+        copy.start()
+        return copy
+
+    base_here = edge_out.at[pl.ds(tiles, layers)]
     edges = []
-    for dy, dx in sides:
-        slot = (1 - dy) * 3 + 1 - dx
-        copy = pltpu.make_async_remote_copy(
-            src_ref=edge_out, dst_ref=edge_in.at[slot],
-            send_sem=edge_send.at[slot], recv_sem=edge_recv.at[slot],
-            device_id=neighbour(dy, dx), device_id_type=MESH,
-        )
-        copy.start()
-        edges.append(copy)
+    for slot, dx in enumerate((1, -1)):
+        edges.append(send(edge_out, edge_in.at[slot], slot, 0, dx))
+    for slot, (dy, dx) in enumerate(((1, 1), (1, -1), (-1, 1), (-1, -1))):
+        edges.append(send(corner_out, corner_in.at[slot], 2 + slot, dy, dx))
+    first, last = pl.ds(0, halo), pl.ds(rows - halo, halo)
+    edges.append(send(base_here.at[:, last], base_in.at[0, :, last], 6, 1, 0))
+    edges.append(send(base_here.at[:, first], base_in.at[1, :, first], 7, -1, 0))
     north = pltpu.make_async_remote_copy(
         src_ref=wide.at[pl.ds(halo, halo)], dst_ref=wide.at[pl.ds(rows + halo, halo)],
         send_sem=row_send.at[0], recv_sem=row_recv.at[0],
@@ -154,24 +180,24 @@
     for copy in edges:
         copy.wait_recv()
 
-    base = [
-        [
-            [base_ref[l] if (y, x) == (1, 1) else edge_in[y * 3 + x, tiles + l] for l in range(layers)]
-            for x in range(3)
-        ]
-        for y in range(3)
-    ]
+    def base_tile(y, x, l):
+        if y == 1:
+            return edge_out[tiles + l] if x == 1 else edge_in[x // 2, tiles + l]
+        if x == 1:
+            return base_in[y // 2, l]
+        return turn(corner_in[y // 2 * 2 + x // 2], -(base_at + l * 2 * halo + halo))
+
+    base = [[[base_tile(y, x, l) for l in range(layers)] for x in range(3)] for y in range(3)]
     base_coefficients(base, coef)
 
-    from_east = lax.rem(lane, 2 * halo) >= halo
-    spread = []
-    for y in range(3):
-        merged = []
-        for t in range(tiles):
-            tile = jnp.where(lax.rem(lane8, 2 * halo) >= halo, edge_in[y * 3 + 2, t], edge_in[y * 3, t])
-            for f in range(fold):
-                merged.append(turn(tile, -f * used))
-        spread.append(jnp.concatenate(merged, 0))
+    from_east = lax.rem(lane8, 2 * halo) >= halo
+    merged = []
+    for t in range(tiles):
+        tile = jnp.where(from_east, edge_in[1, t], edge_in[0, t])
+        for f in range(fold):
+            merged.append(turn(tile, -f * used))
+    spread = jnp.concatenate(merged, 0)
+    corners = [jnp.where(from_east, corner_in[2 * y + 1], corner_in[2 * y]) for y in range(2)]
 
     shifted = {}
 
@@ -180,7 +206,12 @@
             own = wide[e, l]
             r = e - halo
             y = 0 if r < 0 else (2 if r >= rows else 1)
-            z = turn(spread[y], -(2 * halo * (l * rows + r % rows) + halo))
+            if y == 1:
+                z = turn(spread, -(2 * halo * (l * rows + r) + halo))
+            else:
+                z = jnp.concatenate(
+                    [turn(corners[y // 2], -(corner_at(y, g, l) + halo)) for g in range(groups)], 0
+                )
             near = (
                 turn(jnp.where(lane == 0, z, own), -1),
                 turn(jnp.where(lane == cols - 1, z, own), 1),
@@ -222,23 +253,29 @@
             result = result + c[5] * (wide[e + 1, 1 - l] - wide[e - 1, 1 - l])
             evolved_ref[r, l] = result
 
+    copies = cols // vectors
+
+    def gram_row(r):
+        slab = jnp.concatenate([evolved_ref[r, l] for l in range(layers)], 1)
+        return lax.dot_general(
+            slab, jnp.concatenate([slab] * copies, 0), (((1,), (1,)), ((), ())),
+            precision=lax.Precision.HIGHEST, preferred_element_type=jnp.float32,
+        )
+
     middle = [r for r in range(halo, rows - halo)]
+    gram = jnp.zeros((vectors, cols), jnp.float32)
     for r in middle:
         evolve_row(r)
+    for r in middle:
+        gram = gram + gram_row(r)
     north.wait_recv()
     south.wait_recv()
     for r in range(rows):
         if r not in middle:
             evolve_row(r)
-
-    copies = cols // vectors
-    gram = jnp.zeros((vectors, cols), jnp.float32)
     for r in range(rows):
-        slab = jnp.concatenate([evolved_ref[r, l] for l in range(layers)], 1)
-        gram = gram + lax.dot_general(
-            slab, jnp.concatenate([slab] * copies, 0), (((1,), (1,)), ((), ())),
-            precision=lax.Precision.HIGHEST, preferred_element_type=jnp.float32,
-        )
+        if r not in middle:
+            gram = gram + gram_row(r)
     tile = gram[0:SUB]
     for g in range(1, groups):
         tile = jnp.where(lane8 >= g * vectors, gram[g * SUB : (g + 1) * SUB], tile)
@@ -303,6 +340,7 @@
 
 def solution(mesh):
     gy, gx = mesh.shape["gy"], mesh.shape["gx"]
+    hbm = pl.BlockSpec(memory_space=pltpu.HBM)
     vmem = pl.BlockSpec(memory_space=pltpu.VMEM)
 
     def local(base_stream, tangent_vectors):
@@ -317,17 +355,22 @@
                 jax.ShapeDtypeStruct((rows, layers, vectors, cols), f32),
                 jax.ShapeDtypeStruct((SUB, cols), f32),
             ),
-            in_specs=[vmem, vmem],
+            in_specs=[hbm, hbm],
             out_specs=(vmem, vmem),
             scratch_shapes=[
+                pltpu.VMEM((vectors * layers * rows, cols), f32),
                 pltpu.VMEM((rows + 2 * halo, layers, vectors, cols), f32),
                 pltpu.VMEM((6, layers, rows, cols), f32),
                 pltpu.VMEM(edge, f32),
-                pltpu.VMEM((9,) + edge, f32),
+                pltpu.VMEM((2,) + edge, f32),
+                pltpu.VMEM((SUB, cols), f32),
+                pltpu.VMEM((4, SUB, cols), f32),
+                pltpu.VMEM((2, layers, rows, cols), f32),
                 pltpu.VMEM((SUB, cols), f32),
                 pltpu.VMEM((count, SUB, cols), f32),
-                pltpu.SemaphoreType.DMA((9,)),
-                pltpu.SemaphoreType.DMA((9,)),
+                pltpu.SemaphoreType.DMA((2,)),
+                pltpu.SemaphoreType.DMA((8,)),
+                pltpu.SemaphoreType.DMA((8,)),
                 pltpu.SemaphoreType.DMA((2,)),
                 pltpu.SemaphoreType.DMA((2,)),
                 pltpu.SemaphoreType.DMA((count,)),

time: 24.5 us -> 22.8 us (0.931)
  Pallas kernels: 22 us -> 20.3 us
    pallas_call x1, Pallas kernels: 18.1 us -> 16.4 us  [local(): pl.pallas_call(functools.partial(evolve_kernel, gy, gx), out_shape=(jax.S...]
where the time goes in v2:
time: 22.8 us; the launch traced here: 22.5 us
  Pallas kernels  20.3 us (89%)
  local copies, waits for them, and re-layouts  1.64 us (7%)
  between operations  0.65 us (3%)
    pallas_call x1, Pallas kernels, local(): pl.pallas_call(functools.partial(evolve_kernel, gy, gx), out_shape=(jax.S...  16.4 us
    pallas_call x1, Pallas kernels, local(): pl.pallas_call(basis_kernel, out_shape=(jax.ShapeDtypeStruct((vectors * l...  3.82 us
    unnamed x4, local copies, waits for them, and re-layouts  1.64 us

profile of v2, /device:TPU:0, one launch (start us, length us, event | category | flops | bytes accessed | tf_op | source)
XLA Modules:
  0.0 22.5 jit_solution(8318043868213563503)
XLA Ops:
  0.6 0.0 copy-start
  0.6 0.9 %copy-done = f32[32,2,8,128]{3,2,1,0:T(8,128)S(1)} copy-done((f32[32,2,8,128]{3,2,1,0:T(8,128)S(1)}, f32[32,2,8,128]{3,2,1,0:T(8,128)}, u32[]{:S(2)}) %copy-start) | copy-done | bytes 262168
  1.6 0.0 copy-start.1
  1.6 0.7 %copy-done.1 = f32[2,8,128]{2,1,0:T(8,128)S(1)} copy-done((f32[2,8,128]{2,1,0:T(8,128)S(1)}, f32[2,8,128]{2,1,0:T(8,128)}, u32[]{:S(2)}) %copy-start.1) | copy-done | bytes 8216
  2.3 16.4 %evolve.1 = (f32[8,2,32,128]{3,2,1,0:T(8,128)S(1)}, f32[8,128]{1,0:T(8,128)S(1)}) custom-call(f32[2,8,128]{2,1,0:T(8,128)S(1)} %copy-done.1, f32[512,128]{1,0:T(8,128)S(1)} %bitcast.2), custom_call_target="tpu_custom_call" | custom-call | tf_op jit(solution)/shard_map/evolve/pallas_call | solution.py:352
  18.7 3.8 %basis.1 = (f32[512,128]{1,0:T(8,128)}, f32[32,32]{1,0:T(8,128)}) custom-call(f32[8,128]{1,0:T(8,128)S(1)} %get-tuple-element.6.gram_ref, f32[8,2,32,128]{3,2,1,0:T(8,128)S(1)} %get-tuple-element.7.evolved_ref), custom_call_target="tpu_custom_call" | custom-call | tf_op jit(solution)/shard_map/basis/pallas_call | solution.py:384
Async XLA Ops:
  0.6 1.0 %copy-start = (f32[32,2,8,128]{3,2,1,0:T(8,128)S(1)}, f32[32,2,8,128]{3,2,1,0:T(8,128)}, u32[]{:S(2)}) copy-start(f32[32,2,8,128]{3,2,1,0:T(8,128)} %param.3) | copy-start | bytes 786436
  1.6 0.7 %copy-start.1 = (f32[2,8,128]{2,1,0:T(8,128)S(1)}, f32[2,8,128]{2,1,0:T(8,128)}, u32[]{:S(2)}) copy-start(f32[2,8,128]{2,1,0:T(8,128)} %base_ref.1) | copy-start | bytes 24580

commit v3 on v2

--- a/solution.py
+++ b/solution.py
@@ -318,10 +318,64 @@
     work = jnp.concatenate([turn(tile, -g * vectors) for g in range(groups)], 0)
     lane, row = lanes_of((vectors, cols)), rows_of((vectors, cols))
     work = jnp.where(lane < vectors, work, jnp.where(lane == row + vectors, 1.0, 0.0))
-    for j in range(vectors):
-        line = work[j : j + 1]
-        scaled = line / work[j : j + 1, j : j + 1]
-        work = work - jnp.where(row > j, work[:, j : j + 1], 0.0) * scaled
+    def splat(v, j):
+        return jnp.broadcast_to(v[:, j : j + 1], v.shape)
+
+    part = [work[g * SUB : (g + 1) * SUB] for g in range(groups)]
+    row8 = rows_of((SUB, cols))
+    for j in range(0, vectors - 4, 4):
+        home, at = j // SUB, j % SUB
+        line = [jnp.broadcast_to(part[home][at + i : at + i + 1], (SUB, cols)) for i in range(4)]
+        block = [[splat(line[i], j + k) for k in range(4)] for i in range(4)]
+        for i in (0, 2):
+            p, q, s = block[i][i], block[i][i + 1], block[i + 1][i + 1]
+            scale = 1.0 / (p * s - q * q)
+            along = (line[i] * s - line[i + 1] * q) * scale
+            across = (line[i + 1] * p - line[i] * q) * scale
+            if i == 0:
+                pair = {}
+                for k in (2, 3):
+                    pair[k] = (
+                        (block[0][k] * s - block[1][k] * q) * scale,
+                        (block[1][k] * p - block[0][k] * q) * scale,
+                    )
+                upper_rows = [along, across]
+                for m in (2, 3):
+                    line[m] = line[m] - block[0][m] * along - block[1][m] * across
+                fresh = {
+                    (m, k): block[m][k] - block[0][m] * pair[k][0] - block[1][m] * pair[k][1]
+                    for m in (2, 3) for k in (m, 3)
+                }
+                for (m, k), value in fresh.items():
+                    block[m][k] = value
+            else:
+                lower_rows = [along, across]
+        for g in range(home, groups):
+            if g == home and at + 4 == SUB:
+                part[g] = jnp.where(row8 == at + 2, line[2], jnp.where(row8 == at + 3, line[3], part[g]))
+                continue
+            col = [splat(part[g], j + k) for k in range(4)]
+            rest = part[g] - col[0] * upper_rows[0] - col[1] * upper_rows[1]
+            right = [col[k] - col[0] * pair[k][0] - col[1] * pair[k][1] for k in (2, 3)]
+            rest = rest - right[0] * lower_rows[0] - right[1] * lower_rows[1]
+            if g == home:
+                rest = jnp.where(row8 > at + 3, rest, part[g])
+                rest = jnp.where(row8 == at + 2, line[2], jnp.where(row8 == at + 3, line[3], rest))
+            part[g] = rest
+    j = vectors - 4
+    at = SUB - 4
+    first = jnp.broadcast_to(part[-1][at : at + 1], (SUB, cols))
+    second = jnp.broadcast_to(part[-1][at + 1 : at + 2], (SUB, cols))
+    p, q, s = splat(first, j), splat(first, j + 1), splat(second, j + 1)
+    scale = 1.0 / (p * s - q * q)
+    rest = part[-1] - splat(part[-1], j) * ((first * s - second * q) * scale)
+    rest = rest - splat(part[-1], j + 1) * ((second * p - first * q) * scale)
+    part[-1] = jnp.where(row8 > at + 1, rest, part[-1])
+    work = jnp.concatenate(part, 0)
+    above = pltpu.roll(work, 1, 0)
+    pivot = jnp.sum(jnp.where(lane == row - 1, above, 0.0), axis=1, keepdims=True)
+    cross = jnp.sum(jnp.where(lane == row - 1, work, 0.0), axis=1, keepdims=True)
+    work = jnp.where(row % 2 == 1, work - cross / pivot * above, work)
     diagonal = jnp.sum(jnp.where(lane == row, work, 0.0), axis=1, keepdims=True)
     work = work * lax.rsqrt(diagonal)
     upper_ref[...] = jnp.where(lane >= row, work, 0.0)[:, :vectors]
@@ -380,7 +434,7 @@
                 collective_id=0, has_side_effects=True, vmem_limit_bytes=32 * 1024 * 1024
             ),
             name="evolve",
-        )(base_stream, tangent_vectors.reshape(vectors * layers * rows, cols))
+        )(pltpu.with_memory_space_constraint(base_stream, pltpu.HBM), pltpu.with_memory_space_constraint(tangent_vectors.reshape(vectors * layers * rows, cols), pltpu.HBM))
         basis, upper = pl.pallas_call(
             basis_kernel,
             out_shape=(

time: 22.8 us -> 19.8 us (0.87)
  local copies, waits for them, and re-layouts: 1.64 us -> 0 us
  Pallas kernels: 20.3 us -> 19 us
    unnamed x4 -> x0, local copies, waits for them, and re-layouts: 1.64 us -> none
    pallas_call x1, Pallas kernels: 3.82 us -> 2.5 us  [local(): pl.pallas_call(basis_kernel, out_shape=(jax.ShapeDtypeStruct((vectors * l...]
where the time goes in v3:
time: 19.8 us; the launch traced here: 19.6 us
  Pallas kernels  19 us (96%)
  between operations  0.64 us (3%)
    pallas_call x1, Pallas kernels, local(): pl.pallas_call(functools.partial(evolve_kernel, gy, gx), out_shape=(jax.S...  16.5 us
    pallas_call x1, Pallas kernels, local(): pl.pallas_call(basis_kernel, out_shape=(jax.ShapeDtypeStruct((vectors * l...  2.5 us

profile of v3, /device:TPU:0, one launch (start us, length us, event | category | flops | bytes accessed | tf_op | source)
XLA Modules:
  0.0 19.6 jit_solution(10844703942659166871)
XLA Ops:
  0.6 16.5 %evolve.1 = (f32[8,2,32,128]{3,2,1,0:T(8,128)S(1)}, f32[8,128]{1,0:T(8,128)S(1)}) custom-call(f32[2,8,128]{2,1,0:T(8,128)} %base_ref.1, f32[512,128]{1,0:T(8,128)} %bitcast.2), custom_call_target="tpu_custom_call" | custom-call | tf_op jit(solution)/shard_map/evolve/pallas_call | solution.py:406
  17.1 2.5 %basis.1 = (f32[512,128]{1,0:T(8,128)}, f32[32,32]{1,0:T(8,128)}) custom-call(f32[8,128]{1,0:T(8,128)S(1)} %get-tuple-element.6.gram_ref, f32[8,2,32,128]{3,2,1,0:T(8,128)S(1)} %get-tuple-element.7.evolved_ref), custom_call_target="tpu_custom_call" | custom-call | tf_op jit(solution)/shard_map/basis/pallas_call | solution.py:438
